TPU v7x, 256 devices: a whole 4x4x8 slice. The times are simulated.
256 devices in a mesh: grp: 4 (over y), ep: 64 (over x, z, core).
Axes of the slice: x: 4, y: 4, z: 8, core: 2. Of those that a mesh axis runs over, the one named last changes fastest.
Arguments:
- layer_input: bfloat16 [65536, 8192], P(('grp', 'ep')), may hold values from -6 to 6
- output_grad: bfloat16 [65536, 8192], P(('grp', 'ep')), may hold values from -0.119628906 to 0.119628906
- adapter_ids: int32 [65536, 1], P(('grp', 'ep')), may hold values from 0 to 63; in each aligned block of 256 rows (0 to 255, 256 to 511, ...) at most 8 rows name the same one
- owner_map: int32 [64], replicated, may hold values from 0 to 63, each once
- weights: bfloat16 [64, 2, 64, 8192], P('ep', None, None, 'grp'), may hold values from -0.0625 to 0.0625
- moment: float32 [64, 2, 64, 8192], P('ep', None, None, 'grp'), may hold values from -1.8 to 1.8
- second: float32 [64, 2, 64, 8192], P('ep', None, None, 'grp'), may hold values from 0.0002 to 0.004
Outputs:
- moment_next: float32 [64, 2, 64, 8192], P('ep', None, None, 'grp')
- second_next: float32 [64, 2, 64, 8192], P('ep', None, None, 'grp')
- direction: float32 [64, 2, 64, 8192], P('ep', None, None, 'grp')
Inputs may be any that keep to these rules, and one draw needn't show every extreme that they name: `adapter_ids`: among the rows of one device no adapter appears more than 8 times, and some adapter appears exactly 8 times. `owner_map`: each owner index appears once.
All inputs are finite; a program needn't handle non-finite values.
Results may differ from a plain program's by a relative error of at most 0.0026.
Values may be sent and summed in bfloat16 or wider, within the bound.
A program may use at most 128 MiB of HBM per device.

v0:
```python
import jax
import jax.numpy as jnp
from jax import lax
from jax.sharding import PartitionSpec as P

STEP = 100
ADAPTER_SCALING = 2.0
BETA_FIRST = 0.9
BETA_SECOND = 0.999
ADAM_EPSILON = 1e-08


def pack_slots(values, matcher, owner_count, capacity):
    packed = jnp.dot(matcher, values, preferred_element_type=jnp.float32).astype(jnp.bfloat16)
    return packed.reshape(owner_count, capacity, values.shape[1])


def outer_sums(reduced_input, reduced_gradient, input_rows, incoming_gradients):
    down_gradient = lax.dot_general(
        reduced_gradient, input_rows, (((0,), (0,)), ((), ())), preferred_element_type=jnp.float32
    )
    up_gradient = lax.dot_general(
        reduced_input,
        incoming_gradients,
        (((0,), (0,)), ((), ())),
        preferred_element_type=jnp.float32,
    )
    return ADAPTER_SCALING * jnp.stack([down_gradient, up_gradient])


def adam_step(grads, moment, second):
    moment_next = BETA_FIRST * moment + (1.0 - BETA_FIRST) * grads
    second_next = BETA_SECOND * second + (1.0 - BETA_SECOND) * grads * grads
    first_fix = 1.0 - BETA_FIRST**STEP
    second_fix = 1.0 - BETA_SECOND**STEP
    direction = moment_next / first_fix / (jnp.sqrt(second_next / second_fix) + ADAM_EPSILON)
    return (moment_next, second_next, direction)


def per_device(layer_input, output_grad, adapter_ids, owner_map, weights, moment, second):
    owner_count = lax.axis_size("ep")
    row_count = layer_input.shape[0]
    width = layer_input.shape[1]
    capacity = 2 * row_count // owner_count
    adapter_hot = (adapter_ids == jnp.arange(owner_map.shape[0], dtype=jnp.int32)[None, :]).astype(
        jnp.int32
    )
    owner_of = jnp.sum(adapter_hot * owner_map[None, :], axis=1)
    owner_hot = (owner_of[:, None] == jnp.arange(owner_count, dtype=jnp.int32)[None, :]).astype(
        jnp.int32
    )
    position = jnp.sum((jnp.cumsum(owner_hot, axis=0) - 1) * owner_hot, axis=1)
    slot_index = owner_of * capacity + position
    matcher = (
        jnp.arange(owner_count * capacity, dtype=jnp.int32)[:, None] == slot_index[None, :]
    ).astype(jnp.bfloat16)
    input_slots = pack_slots(layer_input, matcher, owner_count, capacity)
    grad_slots = pack_slots(output_grad, matcher, owner_count, capacity)
    recv_input, recv_grad = (
        lax.all_to_all(input_slots, "ep", split_axis=0, concat_axis=0, tiled=True),
        lax.all_to_all(grad_slots, "ep", split_axis=0, concat_axis=0, tiled=True),
    )
    whole = lax.all_gather(weights, "grp", axis=3, tiled=True)
    recv_input = recv_input.reshape(-1, width)
    recv_grad = recv_grad.reshape(-1, width)
    reduced_input = jnp.dot(recv_input, whole[0, 0].T, preferred_element_type=jnp.float32).astype(
        jnp.bfloat16
    )
    reduced_gradient = jnp.dot(recv_grad, whole[0, 1].T, preferred_element_type=jnp.float32).astype(
        jnp.bfloat16
    )
    partial_grads = outer_sums(reduced_input, reduced_gradient, recv_input, recv_grad)
    grads = lax.psum_scatter(partial_grads[None], "grp", scatter_dimension=3, tiled=True)
    return adam_step(grads, moment, second)


def solution(mesh):
    placed = (
        P(("grp", "ep"), None),
        P(("grp", "ep"), None),
        P(("grp", "ep"), None),
        P(),
        P("ep", None, None, "grp"),
        P("ep", None, None, "grp"),
        P("ep", None, None, "grp"),
    )
    return jax.shard_map(
        per_device,
        mesh=mesh,
        in_specs=placed,
        out_specs=(
            P("ep", None, None, "grp"),
            P("ep", None, None, "grp"),
            P("ep", None, None, "grp"),
        ),
        check_vma=False,
    )
```

profile of v0, /device:TPU:1, one launch (start us, length us, event | category | flops | bytes accessed | tf_op | source)
XLA Modules:
  0.0 493.1 jit_solution(13080129072405434227)
XLA Ops:
  7.2 0.8 select_reduce_fusion
  8.0 0.6 reduce-window.6
  8.6 0.2 slice_reduce_fusion
  8.8 0.1 fusion.22
  8.9 7.7 %fusion = bf16[64,8,8192]{2,1,0:T(8,128)(2,1)} fusion(bf16[256,8192]{1,0:T(8,128)(2,1)} %param.8, s32[256]{0:T(256)S(1)} %multiply_add_fusion.1), kind=kOutput, calls=%fused_computation.2 | convolution fusion | flops 2151809024 | bytes 12583936 | tf_op jit(solution)/shard_map/dot_general | solution.py:14
  16.7 13.2 %all-to-all-start = ((bf16[64,8,8192]{2,1,0:T(8,128)(2,1)}), bf16[64,8,8192]{2,1,0:T(8,128)(2,1)}, u32[]{:S(2)}, u32[]{:S(2)}) async-start(bf16[64,8,8192]{2,1,0:T(8,128)(2,1)} %fusion), calls=%async_computation | async-start | bytes 16777216 | tf_op jit(solution)/shard_map/all_to_all | solution.py:61
  29.8 7.7 %fusion.1 = bf16[64,8,8192]{2,1,0:T(8,128)(2,1)} fusion(bf16[256,8192]{1,0:T(8,128)(2,1)} %param.7, s32[256]{0:T(256)S(1)} %multiply_add_fusion.1), kind=kOutput, calls=%fused_computation.3 | convolution fusion | flops 2151809024 | bytes 12583936 | tf_op jit(solution)/shard_map/dot_general | solution.py:14
  37.6 178.0 %all-to-all-done = bf16[64,8,8192]{2,1,0:T(8,128)(2,1)} async-done(((bf16[64,8,8192]{2,1,0:T(8,128)(2,1)}), bf16[64,8,8192]{2,1,0:T(8,128)(2,1)}, u32[]{:S(2)}, u32[]{:S(2)}) %all-to-all-start) | async-done | bytes 8388640 | tf_op jit(solution)/shard_map/all_to_all | solution.py:61
  215.6 6.1 %all-to-all-start.1 = ((bf16[64,8,8192]{2,1,0:T(8,128)(2,1)}), bf16[64,8,8192]{2,1,0:T(8,128)(2,1)}, u32[]{:S(2)}, u32[]{:S(2)}) async-start(bf16[64,8,8192]{2,1,0:T(8,128)(2,1)} %fusion.1), calls=%async_computation.1 | async-start | bytes 16777216 | tf_op jit(solution)/shard_map/all_to_all | solution.py:60
  221.7 0.0 all-gather.2.cloned.1.call-start
  221.8 0.7 all-gather.2.cloned.1.call-update
  222.4 0.2 reduce-scatter.2.cloned.1.call-start
  222.7 36.3 %all-gather.2.cloned.1.call-done = bf16[1,2,64,8192]{3,2,1,0:T(8,128)(2,1)} async-done(((bf16[1,2,64,2048]{3,2,1,0:T(8,128)(2,1)}), bf16[1,2,64,8192]{3,2,1,0:T(8,128)(2,1)}) %all-gather.2.cloned.1.call-update) | async-done | bytes 2097168 | tf_op jit(solution)/shard_map/all_gather | solution.py:63
  258.9 148.5 %all-to-all-done.1 = bf16[64,8,8192]{2,1,0:T(8,128)(2,1)} async-done(((bf16[64,8,8192]{2,1,0:T(8,128)(2,1)}), bf16[64,8,8192]{2,1,0:T(8,128)(2,1)}, u32[]{:S(2)}, u32[]{:S(2)}) %all-to-all-start.1) | async-done | bytes 8388640 | tf_op jit(solution)/shard_map/all_to_all | solution.py:60
  407.5 11.9 %convolution_bitcast_fusion.1 = f32[1,1,64,8192]{3,2,1,0:T(8,128)S(1)} fusion(bf16[64,8,8192]{2,1,0:T(8,128)(2,1)} %all-to-all-done.1, bf16[64,8,8192]{2,1,0:T(8,128)(2,1)} %all-to-all-done, bf16[1,2,64,8192]{3,2,1,0:T(8,128)(2,1)} %all-gather.2.cloned.1.call-done), kind=kOutput, calls=%fused_computation.5 | convolution fusion | flops 1073774592 | bytes 19922944 | tf_op jit(solution)/shard_map/dot_general | solution.py:19
  419.4 13.3 %convolution_bitcast_fusion = f32[1,1,64,8192]{3,2,1,0:T(8,128)} fusion(bf16[64,8,8192]{2,1,0:T(8,128)(2,1)} %all-to-all-done, bf16[64,8,8192]{2,1,0:T(8,128)(2,1)} %all-to-all-done.1, bf16[1,2,64,8192]{3,2,1,0:T(8,128)(2,1)} %all-gather.2.cloned.1.call-done), kind=kOutput, calls=%fused_computation.4 | convolution fusion | flops 1073774592 | bytes 19922944 | tf_op jit(solution)/shard_map/dot_general | solution.py:22
  432.7 3.9 maximum_multiply_fusion
  436.6 0.0 copy-start
  436.6 0.0 copy-start.1
  436.6 0.0 reduce-scatter.2.cloned.1.call-update
  436.6 46.3 %reduce-scatter.2.cloned.1.call-done = f32[1,2,64,2048]{3,2,1,0:T(8,128)} async-done(((f32[1,2,64,8192]{3,2,1,0:T(8,128)}), f32[1,2,64,2048]{3,2,1,0:T(8,128)}) %reduce-scatter.2.cloned.1.call-update) | async-done | bytes 1048592 | tf_op jit(solution)/shard_map/reduce_scatter | solution.py:73
  483.0 0.0 copy-done
  483.0 0.0 copy-done.1
  483.0 3.3 add_divide_fusion
  (4 shorter events, 0.1 us)
Async XLA Ops:
  16.7 199.0 %all-to-all-start = ((bf16[64,8,8192]{2,1,0:T(8,128)(2,1)}), bf16[64,8,8192]{2,1,0:T(8,128)(2,1)}, u32[]{:S(2)}, u32[]{:S(2)}) async-start(bf16[64,8,8192]{2,1,0:T(8,128)(2,1)} %fusion), calls=%async_computation | async-start | bytes 16777216 | tf_op jit(solution)/shard_map/all_to_all | solution.py:61
  215.6 191.9 %all-to-all-start.1 = ((bf16[64,8,8192]{2,1,0:T(8,128)(2,1)}), bf16[64,8,8192]{2,1,0:T(8,128)(2,1)}, u32[]{:S(2)}, u32[]{:S(2)}) async-start(bf16[64,8,8192]{2,1,0:T(8,128)(2,1)} %fusion.1), calls=%async_computation.1 | async-start | bytes 16777216 | tf_op jit(solution)/shard_map/all_to_all | solution.py:60
  221.7 37.2 %all-gather.2.cloned.1.call-start = ((), (), s32[]{:S(2)}) async-start(), calls=%async_computation.3 | async-start | bytes 2621440 | tf_op jit(solution)/shard_map/all_gather | solution.py:63
  222.4 260.5 %reduce-scatter.2.cloned.1.call-start = ((), (), s32[]{:S(2)}) async-start(), calls=%async_computation.4 | async-start | bytes 5242880 | tf_op jit(solution)/shard_map/reduce_scatter | solution.py:73
  436.6 46.3 %copy-start = (f32[1,2,64,2048]{3,2,1,0:T(8,128)S(1)}, f32[1,2,64,2048]{3,2,1,0:T(8,128)}, u32[]{:S(2)}) copy-start(f32[1,2,64,2048]{3,2,1,0:T(8,128)} %param.13) | copy-start | bytes 3145732
  436.6 46.3 %copy-start.1 = (f32[1,2,64,2048]{3,2,1,0:T(8,128)S(1)}, f32[1,2,64,2048]{3,2,1,0:T(8,128)}, u32[]{:S(2)}) copy-start(f32[1,2,64,2048]{3,2,1,0:T(8,128)} %param.12) | copy-start | bytes 3145732
Sparse Core Ops, SparseCore 0:
  224.4 34.5 all-gather.1
  436.8 46.1 reduce-scatter.1
where the time goes:
time: 493 us
  waiting for transfers between devices  410 us (83%)
  matrix products  40.7 us (8%)
  starting transfers between devices  19.5 us (4%)
  between operations  14.1 us (3%)
  other arithmetic  8.74 us (2%)
    all_to_all x1, waiting for transfers between devices, per_device(): lax.all_to_all(grad_slots, 'ep', split_axis=0, concat_axis=0, tiled=True)  178 us
    all_to_all x1, waiting for transfers between devices, per_device(): lax.all_to_all(input_slots, 'ep', split_axis=0, concat_axis=0, tiled=True)  149 us
    reduce_scatter x1, waiting for transfers between devices, per_device(): lax.psum_scatter(partial_grads[None], 'grp', scatter_dimension=3, tiled=T...  46.3 us
    all_gather x1, waiting for transfers between devices, per_device(): whole = lax.all_gather(weights, 'grp', axis=3, tiled=True)  36.3 us
    dot_general x2, matrix products, pack_slots(): jnp.dot(matcher, values, preferred_element_type=jnp.float32)  15.5 us
    dot_general x1, matrix products, outer_sums(): lax.dot_general(reduced_input, incoming_gradients, (((0,), (0,)), ((), ()...  13.3 us
    all_to_all x1, starting transfers between devices, per_device(): lax.all_to_all(grad_slots, 'ep', split_axis=0, concat_axis=0, tiled=True)  13.2 us
    dot_general x1, matrix products, outer_sums(): lax.dot_general(reduced_gradient, input_rows, (((0,), (0,)), ((), ())), p...  11.9 us
  transfers between devices with their start and end apart: 4, of which 4 were waited for; matrix products, arithmetic and copies ran while one was open for 2% of the time, Pallas kernels for 0%

commit v1 on v0

--- a/solution.py
+++ b/solution.py
@@ -60,7 +60,16 @@
         lax.all_to_all(input_slots, "ep", split_axis=0, concat_axis=0, tiled=True),
         lax.all_to_all(grad_slots, "ep", split_axis=0, concat_axis=0, tiled=True),
     )
-    whole = lax.all_gather(weights, "grp", axis=3, tiled=True)
+    ways = lax.axis_size("grp")
+    up = [(d, (d + 1) % ways) for d in range(ways)]
+    down = [(d, (d - 1) % ways) for d in range(ways)]
+    earlier, later = ([weights], [weights])
+    for _ in range(ways // 2):
+        earlier.append(lax.ppermute(earlier[-1], "grp", up))
+    for _ in range((ways - 1) // 2):
+        later.append(lax.ppermute(later[-1], "grp", down))
+    line = jnp.concatenate([*earlier[::-1], *later[1:]], axis=3)
+    whole = jnp.roll(line, (lax.axis_index("grp") - ways // 2) * weights.shape[3], axis=3)
     recv_input = recv_input.reshape(-1, width)
     recv_grad = recv_grad.reshape(-1, width)
     reduced_input = jnp.dot(recv_input, whole[0, 0].T, preferred_element_type=jnp.float32).astype(

time: 493 us -> 493 us (level)
  waiting for transfers between devices: 410 us -> 399 us
  local copies, waits for them, and re-layouts: 0.2 us -> 6.87 us
    all_gather x1 -> x0, waiting for transfers between devices: 36.3 us -> none  [per_device(): whole = lax.all_gather(weights, 'grp', axis=3, tiled=True)]
    ppermute x0 -> x3, waiting for transfers between devices: none -> 24 us  [the longest x2 24 us: per_device(): earlier.append(lax.ppermute(earlier[-1], 'grp', up))]
    unnamed x4 -> x13, local copies, waits for them, and re-layouts: 0.01 us -> 5.82 us
  transfers between devices with their start and end apart: 4 -> 6, of which waited for: 4 -> 5; matrix products, arithmetic and copies ran while one was open for 2% -> 3% of each run, Pallas kernels for 0% -> 0%
where the time goes in v1:
time: 493 us
  waiting for transfers between devices  399 us (81%)
  matrix products  40.7 us (8%)
  starting transfers between devices  23.4 us (5%)
  between operations  14.1 us (3%)
  other arithmetic  8.74 us (2%)
  local copies, waits for them, and re-layouts  6.87 us (1%)
    all_to_all x1, waiting for transfers between devices, per_device(): lax.all_to_all(grad_slots, 'ep', split_axis=0, concat_axis=0, tiled=True)  178 us
    all_to_all x1, waiting for transfers between devices, per_device(): lax.all_to_all(input_slots, 'ep', split_axis=0, concat_axis=0, tiled=True)  151 us
    reduce_scatter x1, waiting for transfers between devices, per_device(): lax.psum_scatter(partial_grads[None], 'grp', scatter_dimension=3, tiled=T...  46.3 us
    ppermute x2, waiting for transfers between devices, per_device(): earlier.append(lax.ppermute(earlier[-1], 'grp', up))  24 us
    dot_general x2, matrix products, pack_slots(): jnp.dot(matcher, values, preferred_element_type=jnp.float32)  15.5 us
    dot_general x1, matrix products, outer_sums(): lax.dot_general(reduced_input, incoming_gradients, (((0,), (0,)), ((), ()...  13.3 us
    all_to_all x1, starting transfers between devices, per_device(): lax.all_to_all(grad_slots, 'ep', split_axis=0, concat_axis=0, tiled=True)  13.2 us
    dot_general x1, matrix products, outer_sums(): lax.dot_general(reduced_gradient, input_rows, (((0,), (0,)), ((), ())), p...  11.9 us
  transfers between devices with their start and end apart: 6, of which 5 were waited for; matrix products, arithmetic and copies ran while one was open for 3% of the time, Pallas kernels for 0%

profile of v1, /device:TPU:1, one launch (start us, length us, event | category | flops | bytes accessed | tf_op | source)
XLA Modules:
  0.0 493.1 jit_solution(11748900340470379243)
XLA Ops:
  7.2 0.8 select_reduce_fusion
  8.0 0.6 reduce-window.6
  8.6 0.2 slice_reduce_fusion
  8.8 0.1 fusion.22
  8.9 7.7 %fusion = bf16[64,8,8192]{2,1,0:T(8,128)(2,1)} fusion(bf16[256,8192]{1,0:T(8,128)(2,1)} %param.8, s32[256]{0:T(256)S(1)} %multiply_add_fusion.1), kind=kOutput, calls=%fused_computation.2 | convolution fusion | flops 2151809024 | bytes 12583936 | tf_op jit(solution)/shard_map/dot_general | solution.py:14
  16.7 13.2 %all-to-all-start = ((bf16[64,8,8192]{2,1,0:T(8,128)(2,1)}), bf16[64,8,8192]{2,1,0:T(8,128)(2,1)}, u32[]{:S(2)}, u32[]{:S(2)}) async-start(bf16[64,8,8192]{2,1,0:T(8,128)(2,1)} %fusion), calls=%async_computation | async-start | bytes 16777216 | tf_op jit(solution)/shard_map/all_to_all | solution.py:61
  29.8 7.7 %fusion.1 = bf16[64,8,8192]{2,1,0:T(8,128)(2,1)} fusion(bf16[256,8192]{1,0:T(8,128)(2,1)} %param.7, s32[256]{0:T(256)S(1)} %multiply_add_fusion.1), kind=kOutput, calls=%fused_computation.3 | convolution fusion | flops 2151809024 | bytes 12583936 | tf_op jit(solution)/shard_map/dot_general | solution.py:14
  37.6 178.0 %all-to-all-done = bf16[64,8,8192]{2,1,0:T(8,128)(2,1)} async-done(((bf16[64,8,8192]{2,1,0:T(8,128)(2,1)}), bf16[64,8,8192]{2,1,0:T(8,128)(2,1)}, u32[]{:S(2)}, u32[]{:S(2)}) %all-to-all-start) | async-done | bytes 8388640 | tf_op jit(solution)/shard_map/all_to_all | solution.py:61
  215.6 6.1 %all-to-all-start.1 = ((bf16[64,8,8192]{2,1,0:T(8,128)(2,1)}), bf16[64,8,8192]{2,1,0:T(8,128)(2,1)}, u32[]{:S(2)}, u32[]{:S(2)}) async-start(bf16[64,8,8192]{2,1,0:T(8,128)(2,1)} %fusion.1), calls=%async_computation.1 | async-start | bytes 16777216 | tf_op jit(solution)/shard_map/all_to_all | solution.py:60
  221.7 0.0 reduce-scatter.2.cloned.1.call-start
  221.8 1.4 collective-permute-start
  223.1 13.1 %collective-permute-done = bf16[1,2,64,2048]{3,2,1,0:T(8,128)(2,1)S(1)} collective-permute-done((bf16[1,2,64,2048]{3,2,1,0:T(8,128)(2,1)S(1)}, bf16[1,2,64,2048]{3,2,1,0:T(8,128)(2,1)S(1)}, u32[]{:S(2)}, u32[]{:S(2)}) %collective-permute-start) | collective-permute-done | bytes 524320 | tf_op jit(solution)/shard_map/ppermute | solution.py:68
  236.3 0.0 collective-permute-start.1
  236.3 2.7 collective-permute-start.2
  238.9 10.8 %collective-permute-done.1 = bf16[1,2,64,2048]{3,2,1,0:T(8,128)(2,1)S(1)} collective-permute-done((bf16[1,2,64,2048]{3,2,1,0:T(8,128)(2,1)S(1)}, bf16[1,2,64,2048]{3,2,1,0:T(8,128)(2,1)S(1)}, u32[]{:S(2)}, u32[]{:S(2)}) %collective-permute-start.1) | collective-permute-done | bytes 524320 | tf_op jit(solution)/shard_map/ppermute | solution.py:68
  249.8 0.8 constant_dynamic-update-slice_fusion.7
  250.6 0.8 constant_dynamic-update-slice_fusion.6
  251.4 0.8 constant_dynamic-update-slice_fusion.5
  252.3 0.0 collective-permute-done.2
  252.3 0.8 constant_dynamic-update-slice_fusion.4
  253.1 0.8 constant_dynamic-update-slice_fusion.3
  253.9 0.8 constant_dynamic-update-slice_fusion.2
  254.8 0.8 constant_dynamic-update-slice_fusion.1
  255.6 0.9 constant_dynamic-update-slice_fusion
  256.5 151.0 %all-to-all-done.1 = bf16[64,8,8192]{2,1,0:T(8,128)(2,1)} async-done(((bf16[64,8,8192]{2,1,0:T(8,128)(2,1)}), bf16[64,8,8192]{2,1,0:T(8,128)(2,1)}, u32[]{:S(2)}, u32[]{:S(2)}) %all-to-all-start.1) | async-done | bytes 8388640 | tf_op jit(solution)/shard_map/all_to_all | solution.py:60
  407.5 13.3 %convolution_bitcast_fusion = f32[1,1,64,8192]{3,2,1,0:T(8,128)} fusion(bf16[64,8,8192]{2,1,0:T(8,128)(2,1)} %all-to-all-done, bf16[64,8,8192]{2,1,0:T(8,128)(2,1)} %all-to-all-done.1, bf16[1,2,64,16384]{3,2,1,0:T(8,128)(2,1)} %constant_dynamic-update-slice_fusion, s32[]{:T(128)S(6)} %select_n.14), kind=kOutput, calls=%fused_computation.4 | convolution fusion | flops 1073774592 | bytes 19922948 | tf_op jit(solution)/shard_map/dot_general | solution.py:22
  420.8 11.9 %convolution_bitcast_fusion.1 = f32[1,1,64,8192]{3,2,1,0:T(8,128)S(1)} fusion(bf16[64,8,8192]{2,1,0:T(8,128)(2,1)} %all-to-all-done.1, bf16[64,8,8192]{2,1,0:T(8,128)(2,1)} %all-to-all-done, bf16[1,2,64,16384]{3,2,1,0:T(8,128)(2,1)} %constant_dynamic-update-slice_fusion, s32[]{:T(128)S(6)} %add.43, s32[]{:T(128)S(6)} %select_n.14), kind=kOutput, calls=%fused_computation.5 | convolution fusion | flops 1073774592 | bytes 19922952 | tf_op jit(solution)/shard_map/dot_general | solution.py:19
  432.7 3.9 maximum_multiply_fusion
  436.6 0.0 reduce-scatter.2.cloned.1.call-update
  436.6 46.3 %reduce-scatter.2.cloned.1.call-done = f32[1,2,64,2048]{3,2,1,0:T(8,128)} async-done(((f32[1,2,64,8192]{3,2,1,0:T(8,128)}), f32[1,2,64,2048]{3,2,1,0:T(8,128)}) %reduce-scatter.2.cloned.1.call-update) | async-done | bytes 1048592 | tf_op jit(solution)/shard_map/reduce_scatter | solution.py:82
  483.0 0.0 copy-done.2
  483.0 3.3 add_divide_fusion
  (9 shorter events, 0.1 us)
Async XLA Ops:
  16.7 199.0 %all-to-all-start = ((bf16[64,8,8192]{2,1,0:T(8,128)(2,1)}), bf16[64,8,8192]{2,1,0:T(8,128)(2,1)}, u32[]{:S(2)}, u32[]{:S(2)}) async-start(bf16[64,8,8192]{2,1,0:T(8,128)(2,1)} %fusion), calls=%async_computation | async-start | bytes 16777216 | tf_op jit(solution)/shard_map/all_to_all | solution.py:61
  37.6 184.2 %copy-start = (bf16[1,2,64,2048]{3,2,1,0:T(8,128)(2,1)S(1)}, bf16[1,2,64,2048]{3,2,1,0:T(8,128)(2,1)}, u32[]{:S(2)}) copy-start(bf16[1,2,64,2048]{3,2,1,0:T(8,128)(2,1)} %param.11) | copy-start | bytes 1572868
  215.6 191.9 %all-to-all-start.1 = ((bf16[64,8,8192]{2,1,0:T(8,128)(2,1)}), bf16[64,8,8192]{2,1,0:T(8,128)(2,1)}, u32[]{:S(2)}, u32[]{:S(2)}) async-start(bf16[64,8,8192]{2,1,0:T(8,128)(2,1)} %fusion.1), calls=%async_computation.1 | async-start | bytes 16777216 | tf_op jit(solution)/shard_map/all_to_all | solution.py:60
  221.7 261.2 %reduce-scatter.2.cloned.1.call-start = ((), (), s32[]{:S(2)}) async-start(), calls=%async_computation.3 | async-start | bytes 5242880 | tf_op jit(solution)/shard_map/reduce_scatter | solution.py:82
  221.8 14.5 %collective-permute-start = (bf16[1,2,64,2048]{3,2,1,0:T(8,128)(2,1)S(1)}, bf16[1,2,64,2048]{3,2,1,0:T(8,128)(2,1)S(1)}, u32[]{:S(2)}, u32[]{:S(2)}) collective-permute-start(bf16[1,2,64,2048]{3,2,1,0:T(8,128)(2,1)S(1)} %copy-done), channel_id=1, source_target_pairs={{0,64},{64,128},{128,192},{192,0},{1,65},{65,129},{129,193},{193,1... | collective-permute-start | bytes 1572872 | tf_op jit(solution)/shard_map/ppermute | solution.py:68
  236.3 13.5 %collective-permute-start.1 = (bf16[1,2,64,2048]{3,2,1,0:T(8,128)(2,1)S(1)}, bf16[1,2,64,2048]{3,2,1,0:T(8,128)(2,1)S(1)}, u32[]{:S(2)}, u32[]{:S(2)}) collective-permute-start(bf16[1,2,64,2048]{3,2,1,0:T(8,128)(2,1)S(1)} %collective-permute-done), channel_id=1, source_target_pairs={{0,64},{64,128},{128,192},{192,0},{1,65},{65,129},{129,193},{193,1... | collective-permute-start | bytes 1572872 | tf_op jit(solution)/shard_map/ppermute | solution.py:68
  236.3 16.0 %collective-permute-start.2 = (bf16[1,2,64,2048]{3,2,1,0:T(8,128)(2,1)S(1)}, bf16[1,2,64,2048]{3,2,1,0:T(8,128)(2,1)S(1)}, u32[]{:S(2)}, u32[]{:S(2)}) collective-permute-start(bf16[1,2,64,2048]{3,2,1,0:T(8,128)(2,1)S(1)} %copy-done), channel_id=1, source_target_pairs={{0,192},{64,0},{128,64},{192,128},{1,193},{65,1},{129,65},{193,129... | collective-permute-start | bytes 1572872 | tf_op jit(solution)/shard_map/ppermute | solution.py:70
  436.6 46.3 %copy-start.1 = (f32[1,2,64,2048]{3,2,1,0:T(8,128)S(1)}, f32[1,2,64,2048]{3,2,1,0:T(8,128)}, u32[]{:S(2)}) copy-start(f32[1,2,64,2048]{3,2,1,0:T(8,128)} %param.13) | copy-start | bytes 3145732
  436.6 46.4 %copy-start.2 = (f32[1,2,64,2048]{3,2,1,0:T(8,128)S(1)}, f32[1,2,64,2048]{3,2,1,0:T(8,128)}, u32[]{:S(2)}) copy-start(f32[1,2,64,2048]{3,2,1,0:T(8,128)} %param.12) | copy-start | bytes 3145732
Sparse Core Ops, SparseCore 0:
  436.8 46.1 reduce-scatter.1
